TPU v7x, 32 devices: a whole 2x2x4 slice. The times are simulated.
32 devices in a mesh: dp: 8 (over z, x), group: 4 (over y, core).
Axes of the slice: x: 2, y: 2, z: 4, core: 2. Of those that a mesh axis runs over, the one named last changes fastest.
Arguments:
- fine_features: bfloat16 [65536, 128], P(('dp', 'group')), may hold values from -6 to 6
- down_map: int32 [16384, 8], P(('dp', 'group')), may hold values from 0 to 2048, as said below
- neighbours: int32 [16384, 27], P(('dp', 'group')), may hold values from 0 to 512, as said below
- voxel_counts: int32 [32], P(('dp', 'group')), may hold values from 1 to 512, as said below
- down_weight: bfloat16 [8, 128, 256], replicated, may hold values from -0.1875 to 0.1875
- mid_weight: bfloat16 [27, 256, 256], replicated, may hold values from -0.078125 to 0.078125
- out_weight: bfloat16 [27, 256, 256], replicated, may hold values from -0.078125 to 0.078125
- norm_gain: float32 [3, 256], replicated, may hold values from 0.5 to 1.5
- norm_bias: float32 [3, 256], replicated, may hold values from -2 to 2
- cotangent: bfloat16 [16384, 256], P(('dp', 'group')), may hold values from -6 to 6
Outputs:
- features: bfloat16 [16384, 256], P(('dp', 'group'))
- fine_grad: bfloat16 [65536, 128], P(('dp', 'group'))
- down_weight_grad: float32 [8, 128, 256], replicated
- mid_weight_grad: float32 [27, 256, 256], replicated
- out_weight_grad: float32 [27, 256, 256], replicated
- gain_grad: float32 [3, 256], replicated
- bias_grad: float32 [3, 256], replicated
Inputs may be any that keep to these rules, and one draw needn't show every extreme that they name: The live coarse rows of a device are its first voxel_counts rows; one device in every draw has all 512 rows live. `down_map`: entry k of coarse row r of a device is 4 * r + (k mod 4) of that device's fine block or the empty mark 2048; of entries k and k + 4 at most one is not empty; rows that are not live hold only the empty mark. `neighbours`: entries are live rows of the same device's block or the empty mark 512; entry 13 of a live row is the row itself; rows that are not live hold only the empty mark.
All inputs are finite; a program needn't handle non-finite values.
Results may differ from a plain program's by a relative error of at most 0.013.
Values sent between devices are 32-bit elements; how exact they have to be, the bound alone decides.
A program may use at most 128 MiB of HBM per device.

v0:
```python
import functools

import jax
import jax.numpy as jnp
from jax import lax
from jax.experimental import pallas as pl
from jax.experimental.pallas import tpu as pltpu
from jax.sharding import PartitionSpec as P

eps_norm = 1e-05
MESH = pl.DeviceIdType.MESH
GROUP = 3
BLOCK = 256
PAIR = 2
GROUPS = (4, 2, 4)
GAP = 1
LAGS = (0, 1, 2, 3, 5, 7, 8, 10, 11)
RING = 16
CORE_RING = 8


def sigmoid(value):
    return 0.5 + 0.5 * jnp.tanh(0.5 * value)


def silu_slope(value):
    sigma = sigmoid(value)
    return sigma * (1.0 + value * (1.0 - sigma))


def dot(left, right):
    return jnp.dot(left, right, preferred_element_type=jnp.float32)


def dot_last(left, right):
    return lax.dot_general(
        left, right, (((1,), (1,)), ((), ())), preferred_element_type=jnp.float32
    )


def kernel(
    dp_size,
    group_size,
    reduce_here,
    fine_ref,
    down_rows_ref,
    nb_rows,
    count_ref,
    down_hbm,
    mid_hbm,
    out_hbm,
    gain_ref,
    bias_ref,
    cotangent_ref,
    features_ref,
    fine_grad_ref,
    results,
    gain_grad_ref,
    bias_grad_ref,
    w_down,
    w_mid,
    w_out,
    spread_fine,
    cols_down,
    nb_cols,
    pickers,
    columns,
    side_by_side,
    act_one,
    act_one_b,
    act_two_b,
    hid_one,
    hid_two,
    hid_three,
    held,
    grad_hidden,
    source_t,
    pair_source_t,
    grad_act,
    side,
    side_cols,
    nb_own,
    nb_pair,
    swap_out,
    swap_in,
    down_all,
    down_got,
    grads,
    from_core,
    from_first_a,
    from_first_b,
    from_second_a,
    from_second_b,
    from_line,
    near,
    far,
    load_sem,
    sum_send,
    sum_recv,
    swap_send,
    swap_recv,
    near_send,
    near_recv,
    far_send,
    far_recv,
):
    rows, width = cotangent_ref.shape
    offsets = nb_rows.shape[0]
    fine_rows, in_width = fine_ref.shape
    children = fine_rows // rows
    down_offsets = down_rows_ref.shape[0]
    units = (offsets + 1) // 2 * (1 if reduce_here else 2)
    chunks = grads.shape[0]
    dp_me = lax.axis_index("dp")
    group_me = lax.axis_index("group")

    loads = [
        pltpu.make_async_copy(source, target, load_sem.at[at])
        for at, (source, target) in enumerate(
            (
                (down_hbm, w_down),
                (mid_hbm, w_mid.at[pl.ds(0, offsets)]),
                (out_hbm, w_out.at[pl.ds(0, offsets)]),
            )
        )
    ]
    for load in loads:
        load.start()

    direct = reduce_here
    peers = [
        {
            "dp": lax.rem(dp_me + dp_step, dp_size),
            "group": lax.rem(group_me + group_step, group_size),
        }
        for dp_step in reversed(range(dp_size))
        for group_step in reversed(range(group_size))
        if (dp_step or group_step) and (direct or not dp_step or not group_step)
    ]
    barrier = pltpu.get_barrier_semaphore()
    for peer in peers:
        pl.semaphore_signal(barrier, inc=1, device_id=peer, device_id_type=MESH)

    def share(at, axis, me, size, slots, send, recv):
        copies = []
        for step in range(1, size):
            copies.append(
                pltpu.make_async_remote_copy(
                    src_ref=slots.at[at, me],
                    dst_ref=slots.at[at, me],
                    send_sem=send.at[at, step - 1],
                    recv_sem=recv.at[at, step - 1],
                    device_id={axis: lax.rem(me + step, size)},
                    device_id_type=MESH,
                )
            )
        for copy in copies:
            copy.start()
        return copies

    def exchange_direct(at, block, combine, meanwhile):
        me = dp_me * group_size + group_me
        near[at, me] = block
        for peer in peers:
            pltpu.make_async_remote_copy(
                src_ref=near.at[at, me],
                dst_ref=near.at[at, me],
                send_sem=near_send.at[at, 0],
                recv_sem=near_recv.at[at, 0],
                device_id=peer,
                device_id_type=MESH,
            ).start()
        for work in meanwhile:
            if work is not None:
                work()
        others = near.at[at, pl.ds(0, len(peers))]
        for sem in (near_recv, near_send):
            pltpu.make_async_copy(others, others, sem.at[at, 0]).wait()
        return combine([near[at, slot] for slot in range(len(peers) + 1)])

    def exchange(at, block, combine, meanwhile=(None, None)):
        if direct:
            return exchange_direct(at, block, combine, meanwhile)
        near[at, group_me] = block
        copies = share(at, "group", group_me, group_size, near, near_send, near_recv)
        if meanwhile[0] is not None:
            meanwhile[0]()
        for copy in copies:
            copy.wait()
        far[at, dp_me] = combine([near[at, slot] for slot in range(group_size)])
        copies = share(at, "dp", dp_me, dp_size, far, far_send, far_recv)
        if meanwhile[1] is not None:
            meanwhile[1]()
        for copy in copies:
            copy.wait()
        return combine([far[at, slot] for slot in range(dp_size)])

    lanes = width // 2

    def stack(first, second, third):
        filler = jnp.zeros((2, lanes), jnp.float32)
        return jnp.concatenate([first, second, third, filler], axis=0)

    def fold(value):
        return jnp.concatenate([value[:, :lanes], value[:, lanes:]], axis=0)

    def unfold(value):
        return jnp.concatenate([value[0:1], value[1:2]], axis=1)

    def add_all(blocks):
        total = blocks[0]
        for block in blocks[1:]:
            total = total + block
        return total

    def merge_all(blocks):
        count = add_all([block[4:6] for block in blocks])
        center = add_all([block[4:6] * block[0:2] for block in blocks]) / count
        squares = add_all(
            [
                block[2:4] + block[4:6] * (block[0:2] - center) * (block[0:2] - center)
                for block in blocks
            ]
        )
        return stack(center, squares, count)

    count = count_ref[...]
    own_count = jnp.broadcast_to(count.astype(jnp.float32), (1, width))
    live = lax.broadcasted_iota(jnp.int32, (rows, width), 0) < count

    def norm_stats(at, hidden, meanwhile=(None, None)):
        center = jnp.sum(hidden, axis=0, keepdims=True) / own_count
        centered = jnp.where(live, hidden - center, 0.0)
        squares = jnp.sum(centered * centered, axis=0, keepdims=True)
        merged = exchange(
            at, stack(fold(center), fold(squares), fold(own_count)), merge_all, meanwhile
        )
        total = unfold(merged[4:6])
        scale = lax.rsqrt(unfold(merged[2:4]) / total + eps_norm)
        return unfold(merged[0:2]), scale, total

    def norm_grad(at, norm, incoming, normed, scale, total, meanwhile=(None, None)):
        shift_sum = fold(jnp.sum(incoming, axis=0, keepdims=True))
        scale_sum = fold(jnp.sum(incoming * normed, axis=0, keepdims=True))
        summed = exchange(
            at, stack(shift_sum, scale_sum, jnp.zeros_like(shift_sum)), add_all, meanwhile
        )
        shift_sum, scale_sum = unfold(summed[0:2]), unfold(summed[2:4])
        bias_grad_ref[norm : norm + 1, :] = shift_sum
        gain_grad_ref[norm : norm + 1, :] = scale_sum
        hidden_grad = (
            scale
            * gain_ref[norm : norm + 1, :]
            * (incoming - shift_sum / total - normed * (scale_sum / total))
        )
        return jnp.where(live, hidden_grad, 0.0).astype(jnp.bfloat16)

    def pick(mask):
        return jnp.where(mask, jnp.bfloat16(1), jnp.bfloat16(0))

    def counting(shape, axis):
        return lax.broadcasted_iota(jnp.int32, shape, axis).astype(jnp.float32).astype(jnp.bfloat16)

    def place_spread(turn, step):
        picked = dot(pickers[turn, : PAIR * rows, :], held[...]).astype(jnp.bfloat16)
        for part in range(PAIR):
            columns[turn, :, part * width : (part + 1) * width] = picked[
                part * rows : (part + 1) * rows
            ]

    def run_steps(first, last, build, place, use, after):
        build(first % 2, first)

        def one(turn, step, more):
            place(turn, step)
            if more:
                build(1 - turn, step + 1)
            use(turn, step)

        bodies = (last - first - 1) // 2

        def body(at, carry):
            for turn in range(2):
                one((first + turn) % 2, first + 2 * at + turn, True)
            after(first + 2 * at, 2)
            return carry

        lax.fori_loop(0, bodies, body, 0)
        for step in range(first + 2 * bodies, last):
            one(step % 2, step, step + 1 < last)
            after(step, 1)

    def convolve(source, weight, hidden):
        places = counting((rows, BLOCK), 1)
        hidden[...] = jnp.zeros_like(hidden)
        for block in range(2):
            side_by_side[:, block * width : (block + 1) * width] = source[
                block * BLOCK : (block + 1) * BLOCK, :
            ]

        def build(turn, step):
            for part in range(GROUP):
                code = nb_cols[step * GROUP + part]
                wanted = jnp.concatenate([jnp.maximum(code, -1 - code)] * (BLOCK // 128), axis=1)
                pickers[turn, part * rows : (part + 1) * rows, :BLOCK] = pick(wanted == places)

        def use(turn, step):
            weights = weight[pl.ds(step * GROUP, GROUP)].reshape(GROUP * width, width)
            hidden[...] += dot(columns[turn], weights)

        def place(turn, step):
            for part in range(GROUP):
                found = dot(
                    pickers[turn, part * rows : (part + 1) * rows, :BLOCK], side_by_side[...]
                )
                code = nb_cols[step * GROUP + part].astype(jnp.float32)
                second = jnp.concatenate([code] * (width // 128), axis=1) < 0
                columns[turn, :, part * width : (part + 1) * width] = jnp.where(
                    second, found[:, width:], found[:, :width]
                ).astype(jnp.bfloat16)

        run_steps(0, offsets // GROUP, build, place, use, no_slot)

    def build_spread(neighbours, offset_of):
        places = counting((BLOCK, rows), 0)

        def build(turn, step):
            for part in range(PAIR):
                wanted = neighbours[pl.ds(offset_of(PAIR * step + part), 1), :]
                wanted = wanted.astype(jnp.float32)
                for first in range(0, rows, BLOCK):
                    here = jnp.broadcast_to(wanted - first, (16, rows)).astype(jnp.bfloat16)
                    pickers[turn, part * rows + first : part * rows + first + BLOCK, :] = pick(
                        jnp.concatenate([here] * (BLOCK // 16), axis=0) == places
                    )

        return build

    def no_slot(at, count):
        pass

    def own_of(second):
        if not reduce_here:
            return lambda at: at
        extra = 14 * pair if second else 14 - 14 * pair
        return lambda at: 14 * pair + at + (extra - 14 * pair) * (jnp.int32(at) == 13)

    def put(second, at, product, more):
        for part in range(PAIR):
            value = product[:, part * width : (part + 1) * width]
            if not reduce_here:
                unit = pl.multiple_of((units * second + PAIR * at + part) * width, width)
                grads[pl.ds(unit, width), :] = value
                continue
            c, half = at, part
            if second:
                c, half = units // PAIR - 1 + at + part, 1 - part
            if isinstance(at, int) and PAIR * at + part == units - 1:
                empty = pair if second else 1 - pair
                c, half = chunks - 2 + empty, empty
            value = value.reshape(grads.shape[1:4] + (8, width))
            here_rows = pl.ds(8 * half, 8)
            if more:
                value = value + grads[c, :, :, :, here_rows]
            grads[c, :, :, :, here_rows] = value

    def convolve_back(weight, act_grad, second, own_slot, other_slot):
        def use_of(offset_of, weigh):
            def use(turn, step):
                spread = columns[turn, :, : PAIR * width]
                weights = jnp.concatenate(
                    [weight[offset_of(PAIR * step + part)] for part in range(PAIR)], axis=1
                )
                act_grad[...] += dot_last(spread, weights)
                if weigh:
                    put(second, step, dot(source_t[...], spread), False)

            return use

        steps = units // PAIR
        offset_of = own_of(second)
        build = build_spread(nb_own, offset_of)
        run_steps(0, steps, build, place_spread, use_of(offset_of, True), own_slot)
        if reduce_here:
            if second:
                offset_of = lambda at: 14 - 14 * pair + at
            else:
                offset_of = lambda at: 13 - 13 * pair + at + 14 * pair * (jnp.int32(at) == 13)
            build = build_spread(nb_own, offset_of)
            run_steps(0, steps, build, place_spread, use_of(offset_of, False), other_slot)

    def convolve_pair(second, first_step, last_step, at_slot):
        def use(turn, step):
            spread = columns[turn, :, : PAIR * width]
            put(second, step, dot(pair_source_t[...], spread), True)

        build = build_spread(nb_pair, own_of(second))
        run_steps(first_step, last_step, build, place_spread, use, at_slot)

    core, row = lax.rem(group_me, 2), group_me // 2
    column, plane = lax.rem(dp_me, 2), dp_me // 2
    pair, high = lax.rem(plane, 2), plane // 2
    planes = 4
    core_peer = {"group": group_me + 1 - 2 * core}
    row_peer = {"group": group_me + 2 - 4 * row}
    column_peer = {"dp": dp_me + 1 - 2 * column}
    pair_peer = {"dp": dp_me + 2 - 4 * pair}
    cross_peer = {"dp": dp_me + 4 - 8 * high}
    own = pl.ds(2 * core, 2)
    lane_a, lane_b = 2 * core, 2 * core + 1
    kept_row, given_row = pl.ds(2 * row, 2), pl.ds(2 * (1 - row), 2)

    def send(c, stage, source, target, peer):
        turn = lax.rem(c, RING)
        return pltpu.make_async_remote_copy(
            src_ref=source,
            dst_ref=target,
            send_sem=sum_send.at[turn],
            recv_sem=sum_recv.at[turn, stage],
            device_id=peer,
            device_id_type=MESH,
        )

    def copies_of(c, stage, size):
        both, some = pl.ds(PAIR * c, size), pl.ds(0, 8 * size)
        part = grads.at[c, :, :, :, some]

        def landing(ref, at):
            return ref.at[(at, *[slice(None)] * (len(ref.shape) - 3), some)]

        if stage == 0:
            given = part.at[pl.ds(2 * (1 - core), 2)]
            return [send(c, stage, given, landing(from_core, lax.rem(c, CORE_RING)), core_peer)]
        if stage == 1:
            return [
                send(c, stage, part.at[lane_a, 1 - column], landing(from_first_a, c), column_peer),
                send(c, stage, part.at[lane_b, :, given_row], landing(from_first_b, c), row_peer),
            ]
        if stage == 2:
            return [
                send(c, stage, part.at[lane_a, column, given_row], landing(from_second_a, c), row_peer),
                send(c, stage, part.at[lane_b, 1 - column, kept_row], landing(from_second_b, c), column_peer),
            ]
        if stage == 3:
            given = part.at[own, column, 2 * row + 1 - high]
            return [send(c, stage, given, landing(from_line, c), cross_peer)]
        if stage == 4:
            block = results.at[pair, both, own, column, 2 * row + high]
            return [
                send(
                    c,
                    stage,
                    block,
                    block,
                    {"dp": 2 * lax.rem(plane + step, planes) + column},
                )
                for step in range(1, planes)
            ]
        if stage == 5:
            block_a = results.at[:, both, lane_a, column, kept_row]
            block_b = results.at[:, both, lane_b, column, kept_row]
            return [
                send(c, stage, block_a, block_a, row_peer),
                send(c, stage, block_b, block_b, column_peer),
            ]
        if stage == 6:
            block_a = results.at[:, both, lane_a, column]
            block_b = results.at[:, both, lane_b, :, kept_row]
            return [
                send(c, stage, block_a, block_a, column_peer),
                send(c, stage, block_b, block_b, row_peer),
            ]
        block = results.at[:, both, own]
        return [send(c, stage, block, block, core_peer)]

    def wait_bytes(sem, like):
        pltpu.make_async_copy(like, like, sem).wait()

    def wait_arrived(c, stage, size):
        some = pl.ds(0, 8 * size)
        like = (
            from_core.at[0, :, :, :, some],
            grads.at[c, 0, :, :, some],
            grads.at[c, 0, 0, :, some],
            from_line.at[c, :, some],
            results.at[0, pl.ds(0, 3 * size), 0, 0, pl.ds(0, 2)],
            grads.at[c, 0, :, :, some],
            grads.at[c, pl.ds(0, 2), :, :, some],
            grads.at[c, :, :, :, some],
        )[stage]
        wait_bytes(sum_recv.at[lax.rem(c, RING), stage], like)

    def wait_sent(c, size):
        like = results.at[0, pl.ds(0, 23), 0, pl.ds(0, size)]
        wait_bytes(sum_send.at[lax.rem(c, RING)], like)

    def stage_of(c, stage, size=PAIR):
        if stage > 0:
            wait_arrived(c, stage - 1, size)
        some = slice(0, 8 * size)

        def add(lanes, columns_of, rows_of, landed):
            here_rows = (c, lanes, columns_of, rows_of, some)
            grads[here_rows] = grads[here_rows] + landed

        every = slice(None)
        if stage == 1:
            add(own, every, every, from_core[lax.rem(c, CORE_RING), :, :, :, some])
        if stage == 2:
            add(lane_a, column, every, from_first_a[c, :, some])
            add(lane_b, every, kept_row, from_first_b[c, :, :, some])
        if stage == 3:
            add(lane_a, column, kept_row, from_second_a[c, :, some])
            add(lane_b, column, kept_row, from_second_b[c, :, some])
        if stage == 4:
            mine = 2 * row + high
            add(own, column, mine, from_line[c, :, some])
            for unit in range(size):
                results[pair, PAIR * c + unit, own, column, mine] = grads[
                    c, own, column, mine, 8 * unit : 8 * unit + 8
                ]
        if stage < len(LAGS) - 1:
            for copy in copies_of(c, stage, size):
                copy.start()
        else:
            wait_sent(c, size)

    early = units // PAIR - 1

    def slot(at, last=False):
        if not reduce_here:
            return
        for stage, lag in enumerate(LAGS):
            entry = at - lag
            if isinstance(at, int):
                c = entry if entry < early else max(entry - GAP, early - 1)
                if 0 <= entry < chunks - 1 + GAP and (c == entry or entry >= early + GAP):
                    stage_of(c, stage)
                continue
            second = entry >= early + GAP

            @pl.when(
                ((entry >= 0) & (entry < early)) | (second & (entry < chunks - 1 + GAP))
            )
            def _():
                stage_of(entry - GAP * second.astype(jnp.int32), stage)

            if last:

                @pl.when(entry == chunks - 1 + GAP)
                def _():
                    stage_of(chunks - 1, stage, 1)

    def slot_after(at, count, steps_with, first_slot):
        if isinstance(at, int):
            for number, step in enumerate(steps_with):
                if at <= step < at + count:
                    slot(first_slot + number)
            return
        start, end = first_slot, first_slot
        for step in steps_with:
            start = start + (at > step).astype(jnp.int32)
            end = end + (at + count > step).astype(jnp.int32)

        def one(number, carry):
            slot(number)
            return carry

        lax.fori_loop(start, end, one, 0)

    def swap(at, source, target):
        return pltpu.make_async_remote_copy(
            src_ref=source,
            dst_ref=target,
            send_sem=swap_send.at[at],
            recv_sem=swap_recv.at[at],
            device_id=pair_peer,
            device_id_type=MESH,
        )

    def swap_rows(at):
        return swap(at, swap_out.at[at % 2], swap_in.at[at])

    def start_rows(at, value):
        if reduce_here:
            swap_out[at % 2] = value.astype(jnp.float32)
            swap_rows(at).start()

    places = nb_rows[...]
    codes = jnp.where(places < BLOCK, places, jnp.where(places < rows, BLOCK - 1 - places, 4 * BLOCK))
    side[...] = jnp.zeros_like(side)
    side[:offsets, :] = codes.astype(jnp.float32)
    side[offsets : offsets + down_offsets, :] = down_rows_ref[...].astype(jnp.float32)
    side_cols[...] = side[...].T
    nb_own[...] = jnp.full_like(nb_own, rows)
    nb_own[:offsets, :] = nb_rows[...]
    swap_neighbours = swap(4, nb_own, nb_pair)
    for weight in (w_mid, w_out):
        weight[offsets:] = jnp.zeros_like(weight[offsets:])

    spread_fine[...] = fine_ref[...].astype(jnp.float32)
    for k in range(down_offsets):
        child = spread_fine[pl.ds(k % children, rows, stride=children), :]
        there = side_cols[:, offsets + k : offsets + k + 1] < fine_rows
        cols_down[:, k * in_width : (k + 1) * in_width] = jnp.where(there, child, 0.0).astype(
            jnp.bfloat16
        )
    loads[0].wait()
    hid_one[...] = dot(cols_down[...], w_down[...].reshape(down_offsets * in_width, width))

    def spread_neighbours():
        for k in range(offsets):
            nb_cols[k] = jnp.broadcast_to(side_cols[:, k : k + 1], (rows, 128)).astype(jnp.bfloat16)

    pl.semaphore_wait(barrier, len(peers))

    swap_one = swap(0, hid_one, swap_in.at[0])
    swap_two = swap(1, hid_two, swap_in.at[1])

    def start_one():
        swap_neighbours.start()
        swap_one.start()

    def start_two():
        swap_two.start()

    beside = (spread_neighbours, start_one if reduce_here else None)
    center_one, scale_one, total = norm_stats(0, hid_one[...], beside)

    def pre_one(hidden=hid_one):
        normed = (hidden[...] - center_one) * scale_one
        return normed, normed * gain_ref[0:1, :] + bias_ref[0:1, :]

    _, pre = pre_one()
    act_one[...] = jnp.where(live, pre * sigmoid(pre), 0.0)
    act_one_b[...] = act_one[...].astype(jnp.bfloat16)
    loads[1].wait()
    convolve(act_one_b, w_mid, hid_two)
    center_two, scale_two, _ = norm_stats(
        1, hid_two[...], (None, start_two if reduce_here else None)
    )

    def pre_two(hidden=hid_two):
        normed = (hidden[...] - center_two) * scale_two
        return normed, normed * gain_ref[1:2, :] + bias_ref[1:2, :]

    _, pre = pre_two()
    act_two_b[...] = jnp.where(live, pre * sigmoid(pre), 0.0).astype(jnp.bfloat16)
    loads[2].wait()
    convolve(act_two_b, w_out, hid_three)
    def turn_two():
        source_t[...] = act_two_b[...].T

    center_three, scale_three, _ = norm_stats(2, hid_three[...], (turn_two, None))
    normed_three = (hid_three[...] - center_three) * scale_three
    summed = (
        jnp.where(live, normed_three * gain_ref[2:3, :] + bias_ref[2:3, :], 0.0) + act_one[...]
    )
    sigma = sigmoid(summed)
    features_ref[...] = jnp.where(live, summed * sigma, 0.0).astype(jnp.bfloat16)

    def pair_source(swapped, pre_of, source_at):
        swapped.wait()
        _, pre = pre_of(swap_in.at[source_at])
        pair_source_t[...] = (pre * sigmoid(pre)).astype(jnp.bfloat16).T

    def pair_two():
        if reduce_here:
            pair_source(swap_two, pre_two, 1)

    slope = sigma * (1.0 + summed * (1.0 - sigma))
    act_one[...] = jnp.where(live, cotangent_ref[...].astype(jnp.float32) * slope, 0.0)
    grad_hidden[...] = norm_grad(
        3, 2, act_one[...], normed_three, scale_three, total, (pair_two, None)
    )
    start_rows(2, grad_hidden[...])
    held[...] = grad_hidden[...]
    grad_act[...] = jnp.zeros_like(grad_act)
    steps = units // PAIR

    def receive(hidden_at):
        swap_rows(hidden_at).wait()
        held[...] = swap_in[hidden_at].astype(jnp.bfloat16)

    def pair_halves(second, at_slot):
        middle = (steps + 1) // 2
        return (
            lambda: convolve_pair(second, 0, middle, at_slot),
            lambda: convolve_pair(second, middle, steps, at_slot),
        )

    nothing = (None, None)
    convolve_back(w_out, grad_act, 0, no_slot, no_slot)
    normed, pre = pre_two()
    incoming = jnp.where(live, grad_act[...] * silu_slope(pre), 0.0)
    if reduce_here:
        swap_neighbours.wait()
        receive(2)
    after = lambda at, count: slot_after(at, count, (0, 4), 0)
    beside = pair_halves(0, after) if reduce_here else nothing
    grad_hidden[...] = norm_grad(4, 1, incoming, normed, scale_two, total, beside)
    start_rows(3, grad_hidden[...])
    held[...] = grad_hidden[...]
    grad_act[...] = act_one[...]
    source_t[...] = act_one_b[...].T
    convolve_back(
        w_mid,
        grad_act,
        1,
        lambda at, count: slot_after(at, count, (0, 5), 2),
        lambda at, count: slot_after(at, count, (1, 3, 5), 4),
    )
    normed, pre = pre_one()
    incoming = jnp.where(live, grad_act[...] * silu_slope(pre), 0.0)
    if reduce_here:
        pair_source(swap_one, pre_one, 0)
        receive(3)
    after = lambda at, count: slot_after(at, count, (0, 1, 3, 5, 6), 7)
    beside = pair_halves(1, after) if reduce_here else nothing
    grad_hidden[...] = norm_grad(5, 0, incoming, normed, scale_one, total, beside)
    down_rows = down_offsets * in_width
    if reduce_here:
        down_all[...] = dot(cols_down[...].T, grad_hidden[...])
        kept = down_rows // 2
        swap_down = swap(
            5, down_all.at[pl.ds(pl.multiple_of(kept * (1 - pair), kept), kept), :], down_got
        )
        swap_down.start()
    else:
        grads[2 * units * width :, :] = dot(cols_down[...].T, grad_hidden[...])
    slot(12)
    for child in range(children):
        total_child = jnp.zeros((rows, in_width), jnp.float32)
        for k in range(child, down_offsets, children):
            there = side_cols[:, offsets + k : offsets + k + 1] < fine_rows
            total_child += jnp.where(there, dot_last(grad_hidden[...], w_down[k]), 0.0)
        spread_fine[pl.ds(child, rows, stride=children), :] = total_child
    fine_grad_ref[...] = spread_fine[...].astype(jnp.bfloat16)
    slot(13)

    if reduce_here:

        def final(at, carry):
            slot(at, True)
            return carry

        swap_down.wait()
        for part in range(PAIR):
            total_down = (
                down_all[pl.ds(pl.multiple_of(kept * pair + part * width, width), width), :]
                + down_got[part * width : (part + 1) * width, :]
            )
            half = 1 - part
            grads[chunks - 2 + part, :, :, :, 8 * half : 8 * half + 8] = total_down.reshape(
                grads.shape[1:4] + (8, width)
            )
        lax.fori_loop(chunks - 2 + GAP, chunks + GAP + LAGS[-1], final, 0)
    else:
        store = pltpu.make_async_copy(grads, results, load_sem.at[0])
        store.start()
        store.wait()


def place_kernel(
    features_ref,
    fine_grad_ref,
    grads_ref,
    gain_ref,
    bias_ref,
    features_out,
    fine_grad_out,
    grad_down_out,
    grad_mid_out,
    grad_out_out,
    gain_out,
    bias_out,
    sem,
):
    half = grad_mid_out.shape[0] // 2
    moves = []
    for at, target in enumerate((grad_out_out, grad_mid_out)):
        for pair in range(2):
            for first in range(0, half, 3):
                count = min(3, half - first)
                here = grads_ref.at[pair, pl.ds(at * half + first, count)]
                moves.append((here, target.at[pl.ds((half + 1) * pair + first, count)]))
        moves.append((grads_ref.at[1 - at, pl.ds(2 * half, 1)], target.at[pl.ds(half, 1)]))
    for pair in range(2):
        down_units = grad_down_out.shape[0] // 2
        here = grads_ref.at[pair, pl.ds(2 * half + 1, down_units)]
        moves.append((here, grad_down_out.at[pl.ds(pair * down_units, down_units)]))
    copies = [
        pltpu.make_async_copy(source, target, sem.at[at])
        for at, (source, target) in enumerate(moves)
    ]
    for copy in copies:
        copy.start()
    features_out[...] = features_ref[...]
    fine_grad_out[...] = fine_grad_ref[...]
    gain_out[...] = gain_ref[...]
    bias_out[...] = bias_ref[...]
    for copy in copies:
        copy.wait()


def per_device(
    dp_size,
    group_size,
    fine_features,
    down_map,
    neighbours,
    voxel_counts,
    down_weight,
    mid_weight,
    out_weight,
    norm_gain,
    norm_bias,
    cotangent,
):
    rows, width = cotangent.shape
    fine_rows, in_width = fine_features.shape
    offsets = neighbours.shape[1]
    down_offsets = down_map.shape[1]
    f32, bf16, i32 = jnp.float32, jnp.bfloat16, jnp.int32
    vmem = pl.BlockSpec(memory_space=pltpu.VMEM)
    hbm = pl.BlockSpec(memory_space=pl.ANY)
    shape = jax.ShapeDtypeStruct
    reduce_here = dp_size == 8 and group_size == 4
    result = pltpu.VMEM if reduce_here else shape
    near_size, far_size = (dp_size * group_size, 1) if reduce_here else (group_size, dp_size)
    share = 2 if reduce_here else 1
    units = (offsets + 1) // 2 * 2 // share
    all_units = 2 * units + down_offsets * in_width // (share * width)
    grad_rows = all_units * width
    chunks = all_units // PAIR
    padded = (offsets + 1) // 2 * 2
    features, fine_grad, grads, gain_grad, bias_grad = pl.pallas_call(
        functools.partial(kernel, dp_size, group_size, reduce_here),
        out_shape=(
            result((rows, width), bf16),
            result((fine_rows, in_width), bf16),
            pltpu.VMEM((2, all_units, *GROUPS, 8, width), f32)
            if reduce_here
            else shape((grad_rows, width), f32),
            result(norm_gain.shape, f32),
            result(norm_bias.shape, f32),
        ),
        in_specs=[vmem, vmem, vmem, vmem, hbm, hbm, hbm, vmem, vmem, vmem],
        out_specs=(vmem, vmem, vmem if reduce_here else hbm, vmem, vmem),
        scratch_shapes=[
            pltpu.VMEM(down_weight.shape, bf16),
            pltpu.VMEM((padded, width, width), bf16),
            pltpu.VMEM((padded, width, width), bf16),
            pltpu.VMEM((fine_rows, in_width), f32),
            pltpu.VMEM((rows, down_offsets * in_width), bf16),
            pltpu.VMEM((offsets, rows, 128), bf16),
            pltpu.VMEM((2, GROUP * rows, rows), bf16),
            pltpu.VMEM((2, rows, GROUP * width), bf16),
            pltpu.VMEM((BLOCK, 2 * width), bf16),
            pltpu.VMEM((rows, width), f32),
            pltpu.VMEM((rows, width), bf16),
            pltpu.VMEM((rows, width), bf16),
            pltpu.VMEM((rows, width), f32),
            pltpu.VMEM((rows, width), f32),
            pltpu.VMEM((rows, width), f32),
            pltpu.VMEM((rows, width), bf16),
            pltpu.VMEM((rows, width), bf16),
            pltpu.VMEM((width, rows), bf16),
            pltpu.VMEM((width, rows), bf16),
            pltpu.VMEM((rows, width), f32),
            pltpu.VMEM((128, rows), f32),
            pltpu.VMEM((rows, 128), f32),
            pltpu.VMEM((padded, rows), i32),
            pltpu.VMEM((padded, rows), i32),
            pltpu.VMEM((2, rows, width), f32),
            pltpu.VMEM((4, rows, width), f32),
            pltpu.VMEM((down_offsets * in_width, width), f32),
            pltpu.VMEM((down_offsets * in_width // 2, width), f32),
            pltpu.VMEM(
                (chunks, *GROUPS, 8 * PAIR, width) if reduce_here else (grad_rows, width), f32
            ),
            pltpu.VMEM((CORE_RING, 2, *GROUPS[1:], 8 * PAIR, width), f32),
            pltpu.VMEM((chunks, GROUPS[2], 8 * PAIR, width), f32),
            pltpu.VMEM((chunks, GROUPS[1], 2, 8 * PAIR, width), f32),
            pltpu.VMEM((chunks, 2, 8 * PAIR, width), f32),
            pltpu.VMEM((chunks, 2, 8 * PAIR, width), f32),
            pltpu.VMEM((chunks, 2, 8 * PAIR, width), f32),
            pltpu.VMEM((6, near_size, 8, width // 2), f32),
            pltpu.VMEM((6, far_size, 8, width // 2), f32),
            pltpu.SemaphoreType.DMA((3,)),
            pltpu.SemaphoreType.DMA((RING,)),
            pltpu.SemaphoreType.DMA((RING, len(LAGS) - 1)),
            pltpu.SemaphoreType.DMA((6,)),
            pltpu.SemaphoreType.DMA((6,)),
            pltpu.SemaphoreType.DMA((6, group_size - 1)),
            pltpu.SemaphoreType.DMA((6, group_size - 1)),
            pltpu.SemaphoreType.DMA((6, far_size)),
            pltpu.SemaphoreType.DMA((6, far_size)),
        ],
        compiler_params=pltpu.CompilerParams(
            collective_id=0, has_side_effects=True, vmem_limit_bytes=(46 if reduce_here else 60) * 1024 * 1024
        ),
    )(
        fine_features,
        down_map.T,
        neighbours.T,
        voxel_counts.reshape(1, 1),
        down_weight,
        mid_weight,
        out_weight,
        norm_gain,
        norm_bias,
        cotangent,
    )
    if not reduce_here:
        grads = lax.psum(grads, ("dp", "group"))
        middle, end = offsets * width, 2 * padded * width
        grad_out = grads[:middle].reshape(out_weight.shape)
        grad_mid = grads[padded * width : padded * width + middle].reshape(mid_weight.shape)
        grad_down = grads[end:].reshape(down_weight.shape)
        return (features, fine_grad, grad_down, grad_mid, grad_out, gain_grad, bias_grad)
    held = [
        pltpu.with_memory_space_constraint(value, pltpu.VMEM)
        for value in (features, fine_grad, grads, gain_grad, bias_grad)
    ]
    features, fine_grad, grad_down, grad_mid, grad_out, gain_grad, bias_grad = pl.pallas_call(
        place_kernel,
        out_shape=(
            shape(features.shape, bf16),
            shape(fine_grad.shape, bf16),
            shape((down_offsets * in_width // width, *GROUPS, 8, width), f32),
            shape((offsets, *GROUPS, 8, width), f32),
            shape((offsets, *GROUPS, 8, width), f32),
            shape(norm_gain.shape, f32),
            shape(norm_bias.shape, f32),
        ),
        in_specs=[vmem] * 5,
        out_specs=(vmem, vmem, hbm, hbm, hbm, vmem, vmem),
        scratch_shapes=[pltpu.SemaphoreType.DMA((24,))],
        compiler_params=pltpu.CompilerParams(vmem_limit_bytes=8 * 1024 * 1024),
    )(*held)
    grad_down = grad_down.reshape(down_weight.shape)
    grad_mid = grad_mid.reshape(mid_weight.shape)
    grad_out = grad_out.reshape(out_weight.shape)
    return (features, fine_grad, grad_down, grad_mid, grad_out, gain_grad, bias_grad)


def solution(mesh):
    in_specs = (
        P(("dp", "group"), None),
        P(("dp", "group"), None),
        P(("dp", "group"), None),
        P(("dp", "group")),
        P(),
        P(),
        P(),
        P(),
        P(),
        P(("dp", "group"), None),
    )
    out_specs = (P(("dp", "group"), None), P(("dp", "group"), None), P(), P(), P(), P(), P())
    return jax.shard_map(
        functools.partial(per_device, mesh.shape["dp"], mesh.shape["group"]),
        mesh=mesh,
        in_specs=in_specs,
        out_specs=out_specs,
        check_vma=False,
    )
```

profile of v0, /device:TPU:0, one launch (start us, length us, event | category | flops | bytes accessed | tf_op | source)
XLA Modules:
  0.0 182.5 jit_solution(1714945390688906908)
XLA Ops:
  1.3 174.6 %shard_map.153 = (bf16[512,256]{1,0:T(8,128)(2,1)S(1)}, bf16[2048,128]{1,0:T(8,128)(2,1)S(1)}, f32[2,30,4,2,4,8,256]{6,5,4,3,2,1,0:T(8,128)S(1)}, f32[3,256]{1,0:T(4,128)S(1)}, f32[3,256]{1,0:T(4,128)S(1)}) custom-call(bf16[2048,128]{1,0:T(8,128)(2,1)} %fine_ref.1, s32[8,512]{1,0:T(8,128)} %bitcast.8, s32[27,512]{1,0:T(8,128)} %bitcast.7, ...), custom_call_target="tpu_custom_call" | custom-call | tf_op jit(solution)/shard_map/pallas_call | solution.py:837
  175.9 6.4 %shard_map.154 = (bf16[512,256]{1,0:T(8,128)(2,1)}, bf16[2048,128]{1,0:T(8,128)(2,1)}, f32[4,4,2,4,8,256]{5,4,3,2,1,0:T(8,128)}, f32[27,4,2,4,8,256]{5,4,3,2,1,0...) custom-call(bf16[512,256]{1,0:T(8,128)(2,1)S(1)} %get-tuple-element.19.features_ref, ...), custom_call_target="tpu_custom_call" | custom-call | tf_op jit(solution)/shard_map/pallas_call | solution.py:926
where the time goes:
time: 183 us
  Pallas kernels  181 us (99%)
    pallas_call x1, Pallas kernels, per_device(): pl.pallas_call(functools.partial(kernel, dp_size, group_size, reduce_here...  175 us
    pallas_call x1, Pallas kernels, per_device(): pl.pallas_call(place_kernel, out_shape=(shape(features.shape, bf16), shap...  6.42 us

commit v1 on v0

--- a/solution.py
+++ b/solution.py
@@ -51,7 +51,7 @@
     out_hbm,
     gain_ref,
     bias_ref,
-    cotangent_ref,
+    cotangent_hbm,
     features_ref,
     fine_grad_ref,
     results,
@@ -60,6 +60,7 @@
     w_down,
     w_mid,
     w_out,
+    cotangent_ref,
     spread_fine,
     cols_down,
     nb_cols,
@@ -104,7 +105,7 @@
     far_send,
     far_recv,
 ):
-    rows, width = cotangent_ref.shape
+    rows, width = cotangent_hbm.shape
     offsets = nb_rows.shape[0]
     fine_rows, in_width = fine_ref.shape
     children = fine_rows // rows
@@ -121,6 +122,7 @@
                 (down_hbm, w_down),
                 (mid_hbm, w_mid.at[pl.ds(0, offsets)]),
                 (out_hbm, w_out.at[pl.ds(0, offsets)]),
+                (cotangent_hbm, cotangent_ref),
             )
         )
     ]
@@ -224,8 +226,8 @@
         )
         return stack(center, squares, count)
 
-    count = count_ref[...]
-    own_count = jnp.broadcast_to(count.astype(jnp.float32), (1, width))
+    count = count_ref[0]
+    own_count = jnp.full((1, width), count.astype(jnp.float32))
     live = lax.broadcasted_iota(jnp.int32, (rows, width), 0) < count
 
     def norm_stats(at, hidden, meanwhile=(None, None)):
@@ -592,11 +594,7 @@
     side[:offsets, :] = codes.astype(jnp.float32)
     side[offsets : offsets + down_offsets, :] = down_rows_ref[...].astype(jnp.float32)
     side_cols[...] = side[...].T
-    nb_own[...] = jnp.full_like(nb_own, rows)
-    nb_own[:offsets, :] = nb_rows[...]
     swap_neighbours = swap(4, nb_own, nb_pair)
-    for weight in (w_mid, w_out):
-        weight[offsets:] = jnp.zeros_like(weight[offsets:])
 
     spread_fine[...] = fine_ref[...].astype(jnp.float32)
     for k in range(down_offsets):
@@ -618,13 +616,19 @@
     swap_two = swap(1, hid_two, swap_in.at[1])
 
     def start_one():
+        nb_own[...] = jnp.full_like(nb_own, rows)
+        nb_own[:offsets, :] = nb_rows[...]
+        for weight in (w_mid, w_out):
+            weight[offsets:] = jnp.zeros_like(weight[offsets:])
+        if not reduce_here:
+            return
         swap_neighbours.start()
         swap_one.start()
 
     def start_two():
         swap_two.start()
 
-    beside = (spread_neighbours, start_one if reduce_here else None)
+    beside = (start_one, spread_neighbours)
     center_one, scale_one, total = norm_stats(0, hid_one[...], beside)
 
     def pre_one(hidden=hid_one):
@@ -652,6 +656,7 @@
         source_t[...] = act_two_b[...].T
 
     center_three, scale_three, _ = norm_stats(2, hid_three[...], (turn_two, None))
+    loads[3].wait()
     normed_three = (hid_three[...] - center_three) * scale_three
     summed = (
         jnp.where(live, normed_three * gain_ref[2:3, :] + bias_ref[2:3, :], 0.0) + act_one[...]
@@ -823,6 +828,7 @@
     down_offsets = down_map.shape[1]
     f32, bf16, i32 = jnp.float32, jnp.bfloat16, jnp.int32
     vmem = pl.BlockSpec(memory_space=pltpu.VMEM)
+    smem = pl.BlockSpec(memory_space=pltpu.SMEM)
     hbm = pl.BlockSpec(memory_space=pl.ANY)
     shape = jax.ShapeDtypeStruct
     reduce_here = dp_size == 8 and group_size == 4
@@ -845,12 +851,13 @@
             result(norm_gain.shape, f32),
             result(norm_bias.shape, f32),
         ),
-        in_specs=[vmem, vmem, vmem, vmem, hbm, hbm, hbm, vmem, vmem, vmem],
+        in_specs=[vmem, vmem, vmem, smem, hbm, hbm, hbm, vmem, vmem, hbm],
         out_specs=(vmem, vmem, vmem if reduce_here else hbm, vmem, vmem),
         scratch_shapes=[
             pltpu.VMEM(down_weight.shape, bf16),
             pltpu.VMEM((padded, width, width), bf16),
             pltpu.VMEM((padded, width, width), bf16),
+            pltpu.VMEM((rows, width), bf16),
             pltpu.VMEM((fine_rows, in_width), f32),
             pltpu.VMEM((rows, down_offsets * in_width), bf16),
             pltpu.VMEM((offsets, rows, 128), bf16),
@@ -887,7 +894,7 @@
             pltpu.VMEM((chunks, 2, 8 * PAIR, width), f32),
             pltpu.VMEM((6, near_size, 8, width // 2), f32),
             pltpu.VMEM((6, far_size, 8, width // 2), f32),
-            pltpu.SemaphoreType.DMA((3,)),
+            pltpu.SemaphoreType.DMA((4,)),
             pltpu.SemaphoreType.DMA((RING,)),
             pltpu.SemaphoreType.DMA((RING, len(LAGS) - 1)),
             pltpu.SemaphoreType.DMA((6,)),
@@ -904,7 +911,7 @@
         fine_features,
         down_map.T,
         neighbours.T,
-        voxel_counts.reshape(1, 1),
+        voxel_counts,
         down_weight,
         mid_weight,
         out_weight,

time: 183 us -> 183 us (level)
  no operation moved by 1% of the time
where the time goes in v1:
time: 183 us
  Pallas kernels  181 us (99%)
    pallas_call x1, Pallas kernels, per_device(): pl.pallas_call(functools.partial(kernel, dp_size, group_size, reduce_here...  175 us
    pallas_call x1, Pallas kernels, per_device(): pl.pallas_call(place_kernel, out_shape=(shape(features.shape, bf16), shap...  6.42 us

profile of v1, /device:TPU:0, one launch (start us, length us, event | category | flops | bytes accessed | tf_op | source)
XLA Modules:
  0.0 182.5 jit_solution(16266420470642095838)
XLA Ops:
  1.3 174.6 %shard_map.153 = (bf16[512,256]{1,0:T(8,128)(2,1)S(1)}, bf16[2048,128]{1,0:T(8,128)(2,1)S(1)}, f32[2,30,4,2,4,8,256]{6,5,4,3,2,1,0:T(8,128)S(1)}, f32[3,256]{1,0:T(4,128)S(1)}, f32[3,256]{1,0:T(4,128)S(1)}) custom-call(bf16[2048,128]{1,0:T(8,128)(2,1)} %fine_ref.1, s32[8,512]{1,0:T(8,128)} %bitcast.6, s32[27,512]{1,0:T(8,128)} %bitcast.5, ...), custom_call_target="tpu_custom_call" | custom-call | tf_op jit(solution)/shard_map/pallas_call | solution.py:843
  175.9 6.4 %shard_map.154 = (bf16[512,256]{1,0:T(8,128)(2,1)}, bf16[2048,128]{1,0:T(8,128)(2,1)}, f32[4,4,2,4,8,256]{5,4,3,2,1,0:T(8,128)}, f32[27,4,2,4,8,256]{5,4,3,2,1,0...) custom-call(bf16[512,256]{1,0:T(8,128)(2,1)S(1)} %get-tuple-element.19.features_ref, ...), custom_call_target="tpu_custom_call" | custom-call | tf_op jit(solution)/shard_map/pallas_call | solution.py:933

commit v2 on v1

--- a/solution.py
+++ b/solution.py
@@ -181,7 +181,7 @@
         return combine([near[at, slot] for slot in range(len(peers) + 1)])
 
     def exchange(at, block, combine, meanwhile=(None, None)):
-        if direct:
+        if direct and at < 4:
             return exchange_direct(at, block, combine, meanwhile)
         near[at, group_me] = block
         copies = share(at, "group", group_me, group_size, near, near_send, near_recv)
@@ -833,7 +833,7 @@
     shape = jax.ShapeDtypeStruct
     reduce_here = dp_size == 8 and group_size == 4
     result = pltpu.VMEM if reduce_here else shape
-    near_size, far_size = (dp_size * group_size, 1) if reduce_here else (group_size, dp_size)
+    near_size = dp_size * group_size if reduce_here else group_size
     share = 2 if reduce_here else 1
     units = (offsets + 1) // 2 * 2 // share
     all_units = 2 * units + down_offsets * in_width // (share * width)
@@ -893,7 +893,7 @@
             pltpu.VMEM((chunks, 2, 8 * PAIR, width), f32),
             pltpu.VMEM((chunks, 2, 8 * PAIR, width), f32),
             pltpu.VMEM((6, near_size, 8, width // 2), f32),
-            pltpu.VMEM((6, far_size, 8, width // 2), f32),
+            pltpu.VMEM((6, dp_size, 8, width // 2), f32),
             pltpu.SemaphoreType.DMA((4,)),
             pltpu.SemaphoreType.DMA((RING,)),
             pltpu.SemaphoreType.DMA((RING, len(LAGS) - 1)),
@@ -901,8 +901,8 @@
             pltpu.SemaphoreType.DMA((6,)),
             pltpu.SemaphoreType.DMA((6, group_size - 1)),
             pltpu.SemaphoreType.DMA((6, group_size - 1)),
-            pltpu.SemaphoreType.DMA((6, far_size)),
-            pltpu.SemaphoreType.DMA((6, far_size)),
+            pltpu.SemaphoreType.DMA((6, dp_size - 1)),
+            pltpu.SemaphoreType.DMA((6, dp_size - 1)),
         ],
         compiler_params=pltpu.CompilerParams(
             collective_id=0, has_side_effects=True, vmem_limit_bytes=(46 if reduce_here else 60) * 1024 * 1024

time: 183 us -> 182 us (level)
  Pallas kernels: 181 us -> 179 us
where the time goes in v2:
time: 182 us; the launch traced here: 181 us
  Pallas kernels  179 us (98%)
    pallas_call x1, Pallas kernels, per_device(): pl.pallas_call(functools.partial(kernel, dp_size, group_size, reduce_here...  173 us
    pallas_call x1, Pallas kernels, per_device(): pl.pallas_call(place_kernel, out_shape=(shape(features.shape, bf16), shap...  6.42 us

profile of v2, /device:TPU:0, one launch (start us, length us, event | category | flops | bytes accessed | tf_op | source)
XLA Modules:
  0.0 180.9 jit_solution(12159141719678898540)
XLA Ops:
  1.3 173.0 %shard_map.153 = (bf16[512,256]{1,0:T(8,128)(2,1)S(1)}, bf16[2048,128]{1,0:T(8,128)(2,1)S(1)}, f32[2,30,4,2,4,8,256]{6,5,4,3,2,1,0:T(8,128)S(1)}, f32[3,256]{1,0:T(4,128)S(1)}, f32[3,256]{1,0:T(4,128)S(1)}) custom-call(bf16[2048,128]{1,0:T(8,128)(2,1)} %fine_ref.1, s32[8,512]{1,0:T(8,128)} %bitcast.6, s32[27,512]{1,0:T(8,128)} %bitcast.5, ...), custom_call_target="tpu_custom_call" | custom-call | tf_op jit(solution)/shard_map/pallas_call | solution.py:843
  174.3 6.4 %shard_map.154 = (bf16[512,256]{1,0:T(8,128)(2,1)}, bf16[2048,128]{1,0:T(8,128)(2,1)}, f32[4,4,2,4,8,256]{5,4,3,2,1,0:T(8,128)}, f32[27,4,2,4,8,256]{5,4,3,2,1,0...) custom-call(bf16[512,256]{1,0:T(8,128)(2,1)S(1)} %get-tuple-element.19.features_ref, ...), custom_call_target="tpu_custom_call" | custom-call | tf_op jit(solution)/shard_map/pallas_call | solution.py:933

commit v3 on v2

--- a/solution.py
+++ b/solution.py
@@ -14,7 +14,7 @@
 PAIR = 2
 GROUPS = (4, 2, 4)
 GAP = 1
-LAGS = (0, 1, 2, 3, 5, 7, 8, 10, 11)
+LAGS = (0, 1, 2, 4, 6, 8, 9, 11, 12)
 RING = 16
 CORE_RING = 8
 
@@ -712,8 +712,8 @@
         w_mid,
         grad_act,
         1,
-        lambda at, count: slot_after(at, count, (0, 5), 2),
-        lambda at, count: slot_after(at, count, (1, 3, 5), 4),
+        lambda at, count: slot_after(at, count, (0, 3, 5), 2),
+        lambda at, count: slot_after(at, count, (1, 5), 5),
     )
     normed, pre = pre_one()
     incoming = jnp.where(live, grad_act[...] * silu_slope(pre), 0.0)

time: 182 us -> 181 us (level)
  no operation moved by 1% of the time
where the time goes in v3:
time: 181 us
  Pallas kernels  179 us (99%)
    pallas_call x1, Pallas kernels, per_device(): pl.pallas_call(functools.partial(kernel, dp_size, group_size, reduce_here...  173 us
    pallas_call x1, Pallas kernels, per_device(): pl.pallas_call(place_kernel, out_shape=(shape(features.shape, bf16), shap...  6.42 us

profile of v3, /device:TPU:0, one launch (start us, length us, event | category | flops | bytes accessed | tf_op | source)
XLA Modules:
  0.0 180.8 jit_solution(11006870150092578214)
XLA Ops:
  1.3 172.9 %shard_map.153 = (bf16[512,256]{1,0:T(8,128)(2,1)S(1)}, bf16[2048,128]{1,0:T(8,128)(2,1)S(1)}, f32[2,30,4,2,4,8,256]{6,5,4,3,2,1,0:T(8,128)S(1)}, f32[3,256]{1,0:T(4,128)S(1)}, f32[3,256]{1,0:T(4,128)S(1)}) custom-call(bf16[2048,128]{1,0:T(8,128)(2,1)} %fine_ref.1, s32[8,512]{1,0:T(8,128)} %bitcast.6, s32[27,512]{1,0:T(8,128)} %bitcast.5, ...), custom_call_target="tpu_custom_call" | custom-call | tf_op jit(solution)/shard_map/pallas_call | solution.py:843
  174.2 6.4 %shard_map.154 = (bf16[512,256]{1,0:T(8,128)(2,1)}, bf16[2048,128]{1,0:T(8,128)(2,1)}, f32[4,4,2,4,8,256]{5,4,3,2,1,0:T(8,128)}, f32[27,4,2,4,8,256]{5,4,3,2,1,0...) custom-call(bf16[512,256]{1,0:T(8,128)(2,1)S(1)} %get-tuple-element.19.features_ref, ...), custom_call_target="tpu_custom_call" | custom-call | tf_op jit(solution)/shard_map/pallas_call | solution.py:933
